TPU v7x, 128 devices: a whole 4x4x4 slice. The times are simulated.
128 devices in a mesh: tile: 16 (over z, y), seq: 8 (over x, core).
Axes of the slice: x: 4, y: 4, z: 4, core: 2. Of those that a mesh axis runs over, the one named last changes fastest.
Arguments:
- cls_tokens: bfloat16 [16384, 1536], P(('tile', 'seq')), may hold values from -6 to 6
- norm_gain: float32 [1536], replicated, may hold values from 0.5 to 1.5
- w_gate: bfloat16 [1536, 4096], P(None, 'tile'), may hold values from -0.15625 to 0.15625
- w_up: bfloat16 [1536, 4096], P(None, 'tile'), may hold values from -0.15625 to 0.15625
- w_down: bfloat16 [4096, 1536], P('tile'), may hold values from -0.09375 to 0.09375
- layer_scale: float32 [1536], replicated, may hold values from 0.25 to 1.75
- final_gain: float32 [1536], replicated, may hold values from 0.5 to 1.5
- w_embed: bfloat16 [1536, 768], replicated, may hold values from -0.15625 to 0.15625
- dest_pos: int32 [16384], P(('tile', 'seq')), may hold values from 0 to 16383, as said below
- tile_coords: int32 [2, 16384], P(None, ('tile', 'seq')), may hold values from 0 to 999
- attn_gain: float32 [768], replicated, may hold values from 0.5 to 1.5
- w_qkv: bfloat16 [768, 2304], replicated, may hold values from -4 to 4
- offsets: int32 [12], replicated, may hold values from 0 to 15
- w_out: bfloat16 [768, 768], replicated, may hold values from -0.21875 to 0.21875
Outputs:
- slide_out: bfloat16 [16384, 768], P(('tile', 'seq'))
Inputs may be any that keep to these rules, and one draw needn't show every extreme that they name: dest_pos holds each number of 0 to 16383 once; the 128 rows of one device go to the devices of the slide order in groups of 0, 1 or 2 rows a device, some pair carrying 2; every device receives 128 rows, 2 of them from the device 128 / 2 places before it in the slide order, counted round.
All inputs are finite; a program needn't handle non-finite values.
Results may differ from a plain program's by a relative error of at most 0.018.
Values may be sent and summed in bfloat16 or wider, within the bound.
No kernel may reach another device: no remote copies, remote signals or barrier semaphores. Data moves between devices by JAX's collectives and lax.ppermute only.
A program may use at most 128 MiB of HBM per device.

v0:
```python
import jax
import jax.numpy as jnp
from jax import lax
from jax.sharding import PartitionSpec as P

HEAD_COUNT = 12
HEAD_WIDTH = 64
SEGMENT_SPACING = 16


def layer_norm(sender_rows, gain):
    average = jnp.mean(sender_rows, axis=-1, keepdims=True)
    centered = sender_rows - average
    variance = jnp.mean(centered * centered, axis=-1, keepdims=True)
    return centered * lax.rsqrt(variance + 1e-06) * gain


def position_table(coords, hidden_width):
    quarter = hidden_width // 4
    frequency = 1.0 / 10000.0 ** (jnp.arange(quarter).astype(jnp.float32) / quarter)
    along_x = coords[:, 0:1].astype(jnp.float32) * frequency[None, :]
    along_y = coords[:, 1:2].astype(jnp.float32) * frequency[None, :]
    return jnp.concatenate(
        [jnp.sin(along_x), jnp.cos(along_x), jnp.sin(along_y), jnp.cos(along_y)], axis=1
    )


def attend(queries, key_rows, values):
    score_scale = queries.shape[-1] ** (-0.5)
    scores = (
        jnp.einsum("qhd,khd->hqk", queries, key_rows, preferred_element_type=jnp.float32)
        * score_scale
    )
    highest = jnp.max(scores, axis=-1, keepdims=True)
    weights = jnp.exp(scores - highest)
    totals = jnp.sum(weights, axis=-1, keepdims=True)
    mixed_rows = jnp.einsum(
        "hqk,khd->qhd", weights.astype(jnp.bfloat16), values, preferred_element_type=jnp.float32
    )
    result = mixed_rows / jnp.transpose(totals, (1, 0, 2))
    logsum = jnp.transpose((highest + jnp.log(totals))[:, :, 0])
    return (result, logsum)


def body(
    cls_tokens,
    norm_gain,
    w_gate,
    w_up,
    w_down,
    layer_scale,
    final_gain,
    w_embed,
    dest_pos,
    tile_coords,
    attn_gain,
    w_qkv,
    offsets,
    w_out,
):
    resident_rows = cls_tokens.shape[0]
    tokens = cls_tokens.astype(jnp.float32)
    normed = layer_norm(tokens, norm_gain).astype(jnp.bfloat16)
    shard_rows = lax.all_gather(normed, "tile", axis=0, tiled=True)
    gate_proj = jnp.dot(shard_rows, w_gate, preferred_element_type=jnp.float32)
    upward = jnp.dot(shard_rows, w_up, preferred_element_type=jnp.float32)
    hidden = (jax.nn.silu(gate_proj) * upward).astype(jnp.bfloat16)
    projected = lax.psum_scatter(
        jnp.dot(hidden, w_down, preferred_element_type=jnp.float32),
        "tile",
        scatter_dimension=0,
        tiled=True,
    )
    mixed_rows = tokens + layer_scale * projected
    final_rows = layer_norm(mixed_rows, final_gain).astype(jnp.bfloat16)
    embedded = jnp.dot(final_rows, w_embed, preferred_element_type=jnp.float32).astype(jnp.bfloat16)
    hidden_width = embedded.shape[1]
    tile_count = lax.axis_size("tile")
    seq_count = lax.axis_size("seq")
    devices = tile_count * seq_count
    capacity = 2 * max(1, resident_rows // devices)
    target = dest_pos // resident_rows
    row_ids = jnp.arange(resident_rows)
    earlier = (target[:, None] == target[None, :]) & (row_ids[None, :] < row_ids[:, None])
    slot_index = jnp.sum(earlier.astype(jnp.int32), axis=1)
    where_to = target * capacity + slot_index
    payload = jnp.zeros((devices * capacity, hidden_width), jnp.bfloat16).at[where_to].set(embedded)
    meta_rows = jnp.stack([dest_pos, tile_coords[0], tile_coords[1]], axis=1)
    meta_table = jnp.full((devices * capacity, 3), -1, jnp.int32).at[where_to].set(meta_rows)
    received, received_meta = (
        lax.all_to_all(
            payload.reshape(devices, capacity, hidden_width),
            ("tile", "seq"),
            split_axis=0,
            concat_axis=0,
            tiled=True,
        ),
        lax.all_to_all(
            meta_table.reshape(devices, capacity, 3),
            ("tile", "seq"),
            split_axis=0,
            concat_axis=0,
            tiled=True,
        ),
    )
    flat_rows = received.reshape(-1, hidden_width)
    flat_meta = received_meta.reshape(-1, 3)
    is_live = flat_meta[:, 0] >= 0
    local_slot = jnp.where(is_live, flat_meta[:, 0] % resident_rows, resident_rows)
    placed = (
        jnp.zeros((resident_rows, hidden_width), jnp.bfloat16)
        .at[local_slot]
        .set(flat_rows, mode="drop")
    )
    coords = (
        jnp.zeros((resident_rows, 2), jnp.int32).at[local_slot].set(flat_meta[:, 1:], mode="drop")
    )
    seq_in = placed.astype(jnp.float32) + position_table(coords, hidden_width)
    normed_seq = layer_norm(seq_in, attn_gain).astype(jnp.bfloat16)
    qkv = jnp.dot(normed_seq, w_qkv, preferred_element_type=jnp.float32).astype(jnp.bfloat16)
    queries = qkv[:, :hidden_width]
    keys_values = qkv[:, hidden_width:]
    segment_kv = lax.all_gather(keys_values, "seq", axis=0, tiled=True)
    near_out, nearby_logsumexp = attend(
        queries.reshape(resident_rows, HEAD_COUNT, HEAD_WIDTH),
        segment_kv[:, :hidden_width].reshape(-1, HEAD_COUNT, HEAD_WIDTH),
        segment_kv[:, hidden_width:].reshape(-1, HEAD_COUNT, HEAD_WIDTH),
    )
    kept_rows = jnp.arange(SEGMENT_SPACING, dtype=jnp.int32)[:, None] == offsets[None, :]

    def select(sender_rows, stacked_rows):
        head_grouped = sender_rows.reshape(
            resident_rows // SEGMENT_SPACING, SEGMENT_SPACING, stacked_rows, HEAD_COUNT, HEAD_WIDTH
        )
        sampled_rows = jnp.sum(
            jnp.where(
                kept_rows[None, :, None, :, None], head_grouped, jnp.zeros((), sender_rows.dtype)
            ),
            axis=1,
        )
        return sampled_rows.reshape(resident_rows // SEGMENT_SPACING, stacked_rows * hidden_width)

    far_kv = lax.all_gather(select(keys_values, 2), ("tile", "seq"), axis=0, tiled=True)
    far_out, far_lse = attend(
        select(queries, 1).reshape(-1, HEAD_COUNT, HEAD_WIDTH),
        far_kv[:, :hidden_width].reshape(-1, HEAD_COUNT, HEAD_WIDTH),
        far_kv[:, hidden_width:].reshape(-1, HEAD_COUNT, HEAD_WIDTH),
    )
    far_full = jnp.where(kept_rows[None, :, :, None], far_out[:, None], 0.0).reshape(
        resident_rows, HEAD_COUNT, HEAD_WIDTH
    )
    nearby_grouped = nearby_logsumexp.reshape(
        resident_rows // SEGMENT_SPACING, SEGMENT_SPACING, HEAD_COUNT
    )
    far_share = jnp.where(
        kept_rows[None], 1.0 / (1.0 + jnp.exp(nearby_grouped - far_lse[:, None])), 0.0
    ).reshape(resident_rows, HEAD_COUNT)
    combined = (1.0 - far_share)[:, :, None] * near_out + far_share[:, :, None] * far_full
    attn_rows = combined.reshape(resident_rows, hidden_width).astype(jnp.bfloat16)
    return (seq_in + jnp.dot(attn_rows, w_out, preferred_element_type=jnp.float32)).astype(
        jnp.bfloat16
    )


def solution(mesh):
    in_specs = (
        P(("tile", "seq"), None),
        P(),
        P(None, "tile"),
        P(None, "tile"),
        P("tile", None),
        P(),
        P(),
        P(),
        P(("tile", "seq")),
        P(None, ("tile", "seq")),
        P(),
        P(),
        P(),
        P(),
    )
    out_specs = P(("tile", "seq"), None)
    return jax.shard_map(body, mesh=mesh, in_specs=in_specs, out_specs=out_specs, check_vma=False)
```

profile of v0, /device:TPU:1, one launch (start us, length us, event | category | flops | bytes accessed | tf_op | source)
XLA Modules:
  0.0 357.2 jit_solution(11485548192163310712)
XLA Ops:
  6.5 1.3 convert_reduce_fusion
  7.8 1.2 fusion.31
  9.1 2.0 fusion.33
  11.2 64.7 %all-gather.4.cloned.1.call-done = bf16[2048,1536]{1,0:T(8,128)(2,1)} async-done(((bf16[128,1536]{1,0:T(8,128)(2,1)}), bf16[2048,1536]{1,0:T(8,128)(2,1)}) %all-gather.4.cloned.1.call-update) | async-done | bytes 6291472 | tf_op jit(solution)/shard_map/all_gather | solution.py:64
  75.9 6.1 %fusion.70 = f32[2048,256]{1,0:T(8,128)} fusion(bf16[2048,1536]{1,0:T(8,128)(2,1)} %all-gather.4.cloned.1.call-done, bf16[1536,256]{1,0:T(8,128)(2,1)} %param.16), kind=kOutput, calls=%fused_computation.112 | convolution fusion | flops 1610612736 | bytes 9175040 | tf_op jit(solution)/shard_map/dot_general | solution.py:65
  82.0 14.6 %fusion.7 = f32[2048,1536]{1,0:T(8,128)} fusion(bf16[256,1536]{1,0:T(8,128)(2,1)} %param.18, bf16[2048,1536]{1,0:T(8,128)(2,1)} %all-gather.4.cloned.1.call-done, bf16[1536,256]{1,0:T(8,128)(2,1)} %param.17, f32[2048,256]{1,0:T(8,128)} %fusion.70), kind=kOutput, calls=%fused_computation.14 | convolution fusion | flops 3224371200 | bytes 22544384 | tf_op jit(solution)/shard_map/dot_general | solution.py:69
  97.4 1.2 pad_add_fusion
  98.6 1.4 copy.75
  102.0 1.8 scatter_custom_fusion
  103.8 8.3 %all-to-all-start = ((s32[128,2,3]{2,1,0:T(2,128)}), s32[128,2,3]{2,1,0:T(2,128)}, u32[]{:S(2)}, u32[]{:S(2)}) async-start(s32[128,2,3]{2,1,0:T(2,128)} %bitcast.76), calls=%async_computation | async-start | bytes 262144 | tf_op jit(solution)/shard_map/all_to_all | solution.py:98
  112.8 9.2 %all-to-all-done = s32[128,2,3]{2,1,0:T(2,128)} async-done(((s32[128,2,3]{2,1,0:T(2,128)}), s32[128,2,3]{2,1,0:T(2,128)}, u32[]{:S(2)}, u32[]{:S(2)}) %all-to-all-start) | async-done | bytes 3104 | tf_op jit(solution)/shard_map/all_to_all | solution.py:98
  122.0 1.5 copy.93
  123.5 68.9 %reduce-scatter.2.cloned.1.call-done = f32[128,1536]{1,0:T(8,128)} async-done(((f32[2048,1536]{1,0:T(8,128)}), f32[128,1536]{1,0:T(8,128)}) %reduce-scatter.2.cloned.1.call-update) | async-done | bytes 786448 | tf_op jit(solution)/shard_map/reduce_scatter | solution.py:68
  192.4 1.5 fusion.39
  193.9 1.5 multiply_reduce_fusion.1
  195.4 2.9 convolution_convert_fusion.1
  198.3 2.3 scatter_custom_fusion.1
  200.6 1.9 reshape.194
  202.5 7.8 %all-to-all-start.1 = ((bf16[128,2,768]{2,1,0:T(2,128)(2,1)}), bf16[128,2,768]{2,1,0:T(2,128)(2,1)}, u32[]{:S(2)}, u32[]{:S(2)}) async-start(bf16[128,2,768]{2,1,0:T(2,128)(2,1)} %reshape.194), calls=%async_computation.2 | async-start | bytes 786432 | tf_op jit(solution)/shard_map/all_to_all | solution.py:91
  211.0 2.2 scatter_custom_fusion.3
  214.3 2.5 multiply_sine_fusion.1
  216.7 5.6 %all-to-all-done.1 = bf16[128,2,768]{2,1,0:T(2,128)(2,1)} async-done(((bf16[128,2,768]{2,1,0:T(2,128)(2,1)}), bf16[128,2,768]{2,1,0:T(2,128)(2,1)}, u32[]{:S(2)}, u32[]{:S(2)}) %all-to-all-start.1) | async-done | bytes 393248 | tf_op jit(solution)/shard_map/all_to_all | solution.py:91
  222.3 1.9 reshape.224
  224.2 2.7 scatter_custom_fusion.2
  226.9 1.4 fusion.66
  231.0 2.6 reshape.199
  233.5 2.2 select_reduce_fusion
  235.8 1.6 reshape.200
  239.4 1.6 slice.53
  241.1 1.8 copy.81
  242.8 2.1 reshape.198
  244.9 1.9 select_reduce_fusion.1
  246.8 8.7 %all-gather.6.cloned.1.call-done = bf16[1024,1536]{1,0:T(8,128)(2,1)} async-done(((bf16[128,1536]{1,0:T(8,128)(2,1)}), bf16[1024,1536]{1,0:T(8,128)(2,1)}) %all-gather.6.cloned.1.call-update) | async-done | bytes 3145744 | tf_op jit(solution)/shard_map/all_gather | solution.py:123
  255.4 3.8 %fusion.68 = (bf16[1024,768]{1,0:T(8,128)(2,1)}, bf16[1024,768]{1,0:T(8,128)(2,1)}) fusion(bf16[1024,1536]{1,0:T(8,128)(2,1)} %all-gather.6.cloned.1.call-done), kind=kLoop, calls=%fused_computation.110 | loop fusion | bytes 6291456 | tf_op jit(solution)/shard_map/slice | solution.py:126
  259.2 2.6 copy.82
  261.9 2.6 copy.85
  264.5 2.6 multiply_reduce_fusion
  267.1 2.7 copy-done.1
  269.8 1.9 fusion.1
  271.7 52.7 %all-gather.8.cloned.1.call-done = bf16[1024,1536]{1,0:T(8,128)(2,1)} async-done(((bf16[8,1536]{1,0:T(8,128)(2,1)}), bf16[1024,1536]{1,0:T(8,128)(2,1)}) %all-gather.8.cloned.1.call-update) | async-done | bytes 3145744 | tf_op jit(solution)/shard_map/all_gather | solution.py:143
  324.3 3.8 %fusion.67 = (bf16[1024,768]{1,0:T(8,128)(2,1)}, bf16[1024,768]{1,0:T(8,128)(2,1)}) fusion(bf16[1024,1536]{1,0:T(8,128)(2,1)} %all-gather.8.cloned.1.call-done), kind=kLoop, calls=%fused_computation.109 | loop fusion | bytes 6291456 | tf_op jit(solution)/shard_map/slice | solution.py:146
  328.1 2.6 copy.83
  330.7 1.8 fusion.69
  334.8 1.5 sub.78
  336.2 2.6 copy.86
  338.8 2.1 fusion.15
  341.9 2.1 copy.89
  344.8 4.8 %fusion.26 = bf16[128,12,64]{0,2,1:T(8,128)(2,1)S(1)} fusion(bf16[1024,12,64]{0,2,1:T(8,128)(2,1)} %bitcast.74, f32[12,128,1024]{2,1,0:T(8,128)} %copy-done.1, f32[12,128]{1,0:T(8,128)S(1)} %get-tuple-element.23, f32[128,12,64]{0,2,1:T(8,128)} %copy.89, f32[128,12]{0,1:T(8,128)S(1)} %get-tuple-element.8, f32[128,12]{0,1:T(8,128)} %bitcast.79, ...), kind=kOutput, calls=%fused_computation.33 | convolution fusion | flops 206635008 | bytes 8480256 | tf_op jit(solution)/shard_map/hqk,khd->qhd/dot_general | solution.py:37
  (61 shorter events, 14.9 us)
Async XLA Ops:
  6.5 222.0 %copy-start = (bf16[768,2304]{1,0:T(8,128)(2,1)S(1)}, bf16[768,2304]{1,0:T(8,128)(2,1)}, u32[]{:S(2)}) copy-start(bf16[768,2304]{1,0:T(8,128)(2,1)} %param.25) | copy-start | bytes 10616836
  6.5 69.4 %all-gather.4.cloned.1.call-start = ((), (), s32[]{:S(2)}) async-start(), calls=%async_computation.3 | async-start | bytes 6684672 | tf_op jit(solution)/shard_map/all_gather | solution.py:64
  11.1 181.2 %reduce-scatter.2.cloned.1.call-start = ((), (), s32[]{:S(2)}) async-start(), calls=%async_computation.4 | async-start | bytes 13369344 | tf_op jit(solution)/shard_map/reduce_scatter | solution.py:68
  96.6 95.8 %copy-start.9 = (f32[1536]{0:T(1024)S(1)}, f32[1536]{0:T(1024)}, u32[]{:S(2)}) copy-start(f32[1536]{0:T(1024)} %param.19) | copy-start | bytes 18436
  96.6 98.8 %copy-start.11 = (f32[1536]{0:T(1024)S(1)}, f32[1536]{0:T(1024)}, u32[]{:S(2)}) copy-start(f32[1536]{0:T(1024)} %param.20) | copy-start | bytes 18436
  103.8 18.1 %all-to-all-start = ((s32[128,2,3]{2,1,0:T(2,128)}), s32[128,2,3]{2,1,0:T(2,128)}, u32[]{:S(2)}, u32[]{:S(2)}) async-start(s32[128,2,3]{2,1,0:T(2,128)} %bitcast.76), calls=%async_computation | async-start | bytes 262144 | tf_op jit(solution)/shard_map/all_to_all | solution.py:98
  192.4 3.0 copy-start.2
  192.4 3.0 copy-start.3
  200.6 28.0 %copy-start.12 = (f32[768]{0:T(1024)S(1)}, f32[768]{0:T(1024)}, u32[]{:S(2)}) copy-start(f32[768]{0:T(1024)} %param.24) | copy-start | bytes 9220
  202.5 19.8 %all-to-all-start.1 = ((bf16[128,2,768]{2,1,0:T(2,128)(2,1)}), bf16[128,2,768]{2,1,0:T(2,128)(2,1)}, u32[]{:S(2)}, u32[]{:S(2)}) async-start(bf16[128,2,768]{2,1,0:T(2,128)(2,1)} %reshape.194), calls=%async_computation.2 | async-start | bytes 786432 | tf_op jit(solution)/shard_map/all_to_all | solution.py:91
  210.3 45.2 %all-gather.6.cloned.1.call-start = ((), (), s32[]{:S(2)}) async-start(), calls=%async_computation.5 | async-start | bytes 3538944 | tf_op jit(solution)/shard_map/all_gather | solution.py:123
  228.3 0.9 copy-start.4
  228.5 2.4 copy-start.13
  229.2 0.8 copy-start.7
  230.9 93.4 %all-gather.8.cloned.1.call-start = ((), (), s32[]{:S(2)}) async-start(), calls=%async_computation.6 | async-start | bytes 3170304 | tf_op jit(solution)/shard_map/all_gather | solution.py:143
  267.1 2.7 copy-start.1
  332.5 0.7 copy-start.6
  333.5 0.6 copy-start.10
  344.8 4.8 %copy-start.5 = (f32[128,768]{1,0:T(8,128)S(1)}, f32[128,768]{1,0:T(8,128)}, u32[]{:S(2)}) copy-start(f32[128,768]{1,0:T(8,128)} %copy-done.4) | copy-start | bytes 1179652
  344.8 4.8 %copy-start.8 = (bf16[768,768]{1,0:T(8,128)(2,1)S(1)}, bf16[768,768]{1,0:T(8,128)(2,1)}, u32[]{:S(2)}) copy-start(bf16[768,768]{1,0:T(8,128)(2,1)} %param.27) | copy-start | bytes 3538948
Sparse Core Ops, SparseCore 0:
  11.3 64.6 all-gather.3
  96.7 95.5 reduce-scatter.1
  231.0 24.3 all-gather.5
  258.4 65.8 all-gather.7
where the time goes:
time: 358 us; the launch traced here: 357 us
  waiting for transfers between devices  210 us (59%)
  local copies, waits for them, and re-layouts  56.9 us (16%)
  matrix products  36.7 us (10%)
  other arithmetic  24.2 us (7%)
  starting transfers between devices  16.2 us (5%)
  between operations  13.4 us (4%)
    reduce_scatter x1, waiting for transfers between devices, body(): lax.psum_scatter(jnp.dot(hidden, w_down, preferred_element_type=jnp.float...  68.9 us
    all_gather x1, waiting for transfers between devices, body(): shard_rows = lax.all_gather(normed, 'tile', axis=0, tiled=True)  64.7 us
    all_gather x1, waiting for transfers between devices, body(): lax.all_gather(select(keys_values, 2), ('tile', 'seq'), axis=0, tiled=True)  52.7 us
    dot_general x1, matrix products, body(): jnp.dot(hidden, w_down, preferred_element_type=jnp.float32)  14.6 us
    all_to_all x1, waiting for transfers between devices, body(): lax.all_to_all(meta_table.reshape(devices, capacity, 3), ('tile', 'seq'),...  9.2 us
    all_gather x1, waiting for transfers between devices, body(): segment_kv = lax.all_gather(keys_values, 'seq', axis=0, tiled=True)  8.69 us
    all_to_all x1, starting transfers between devices, body(): lax.all_to_all(meta_table.reshape(devices, capacity, 3), ('tile', 'seq'),...  8.32 us
    all_to_all x1, starting transfers between devices, body(): lax.all_to_all(payload.reshape(devices, capacity, hidden_width), ('tile',...  7.79 us
  transfers between devices with their start and end apart: 6, of which 6 were waited for; matrix products, arithmetic and copies ran while one was open for 13% of the time, Pallas kernels for 0%

commit v1 on v0

--- a/solution.py
+++ b/solution.py
@@ -120,7 +120,8 @@
     qkv = jnp.dot(normed_seq, w_qkv, preferred_element_type=jnp.float32).astype(jnp.bfloat16)
     queries = qkv[:, :hidden_width]
     keys_values = qkv[:, hidden_width:]
-    segment_kv = lax.all_gather(keys_values, "seq", axis=0, tiled=True)
+    copies = jnp.concatenate([keys_values] * lax.axis_size("seq"), axis=0)
+    segment_kv = lax.all_to_all(copies, "seq", 0, 0, tiled=True)
     near_out, nearby_logsumexp = attend(
         queries.reshape(resident_rows, HEAD_COUNT, HEAD_WIDTH),
         segment_kv[:, :hidden_width].reshape(-1, HEAD_COUNT, HEAD_WIDTH),

time: 358 us -> 323 us (0.902)
  local copies, waits for them, and re-layouts: 56.9 us -> 38.8 us
  waiting for transfers between devices: 210 us -> 197 us
  other arithmetic: 24.2 us -> 18.5 us
  starting transfers between devices: 16.2 us -> 20.6 us
    all_gather x1, waiting for transfers between devices: 52.7 us -> 10.6 us  [body(): lax.all_gather(select(keys_values, 2), ('tile', 'seq'), axis=0, tiled=True)]
    all_to_all x0 -> x1, waiting for transfers between devices: none -> 34 us  [body(): segment_kv = lax.all_to_all(copies, 'seq', 0, 0, tiled=True)]
    all_gather x1 -> x0, waiting for transfers between devices: 8.69 us -> none  [body(): segment_kv = lax.all_gather(keys_values, 'seq', axis=0, tiled=True)]
    unnamed x29 -> x48, local copies, waits for them, and re-layouts: 6.38 us -> 11.3 us
    slice x2 -> x1, local copies, waits for them, and re-layouts: 6.41 us -> 1.87 us  [body(): segment_kv[:, :hidden_width].reshape(-1, HEAD_COUNT, HEAD_WIDTH)]
    all_to_all x0 -> x1, starting transfers between devices: none -> 4.44 us  [body(): segment_kv = lax.all_to_all(copies, 'seq', 0, 0, tiled=True)]
    reduce_scatter x1, waiting for transfers between devices: 68.9 us -> 73.2 us  [body(): lax.psum_scatter(jnp.dot(hidden, w_down, preferred_element_type=jnp.float...]
  transfers between devices with their start and end apart: 6 -> 6, of which waited for: 6 -> 6; matrix products, arithmetic and copies ran while one was open for 13% -> 7% of each run, Pallas kernels for 0% -> 0%
where the time goes in v1:
time: 323 us; the launch traced here: 322 us
  waiting for transfers between devices  197 us (61%)
  local copies, waits for them, and re-layouts  38.8 us (12%)
  matrix products  34 us (11%)
  starting transfers between devices  20.6 us (6%)
  other arithmetic  18.5 us (6%)
  between operations  13.5 us (4%)
    reduce_scatter x1, waiting for transfers between devices, body(): lax.psum_scatter(jnp.dot(hidden, w_down, preferred_element_type=jnp.float...  73.2 us
    all_gather x1, waiting for transfers between devices, body(): shard_rows = lax.all_gather(normed, 'tile', axis=0, tiled=True)  64.7 us
    all_to_all x1, waiting for transfers between devices, body(): segment_kv = lax.all_to_all(copies, 'seq', 0, 0, tiled=True)  34 us
    dot_general x1, matrix products, body(): jnp.dot(hidden, w_down, preferred_element_type=jnp.float32)  14.6 us
    unnamed x48, local copies, waits for them, and re-layouts  11.3 us
    all_gather x1, waiting for transfers between devices, body(): lax.all_gather(select(keys_values, 2), ('tile', 'seq'), axis=0, tiled=True)  10.6 us
    all_to_all x1, waiting for transfers between devices, body(): lax.all_to_all(meta_table.reshape(devices, capacity, 3), ('tile', 'seq'),...  8.54 us
    all_to_all x1, starting transfers between devices, body(): lax.all_to_all(meta_table.reshape(devices, capacity, 3), ('tile', 'seq'),...  8.32 us
  transfers between devices with their start and end apart: 6, of which 6 were waited for; matrix products, arithmetic and copies ran while one was open for 7% of the time, Pallas kernels for 0%

profile of v1, /device:TPU:1, one launch (start us, length us, event | category | flops | bytes accessed | tf_op | source)
XLA Modules:
  0.0 322.2 jit_solution(10520869918505830723)
XLA Ops:
  6.5 1.3 convert_reduce_fusion
  7.8 1.2 fusion.31
  9.1 2.0 fusion.33
  11.2 64.7 %all-gather.3.cloned.1.call-done = bf16[2048,1536]{1,0:T(8,128)(2,1)} async-done(((bf16[128,1536]{1,0:T(8,128)(2,1)}), bf16[2048,1536]{1,0:T(8,128)(2,1)}) %all-gather.3.cloned.1.call-update) | async-done | bytes 6291472 | tf_op jit(solution)/shard_map/all_gather | solution.py:64
  75.9 6.1 %fusion.71 = f32[2048,256]{1,0:T(8,128)} fusion(bf16[2048,1536]{1,0:T(8,128)(2,1)} %all-gather.3.cloned.1.call-done, bf16[1536,256]{1,0:T(8,128)(2,1)} %param.16), kind=kOutput, calls=%fused_computation.121 | convolution fusion | flops 1610612736 | bytes 9175040 | tf_op jit(solution)/shard_map/dot_general | solution.py:65
  82.0 14.6 %fusion.7 = f32[2048,1536]{1,0:T(8,128)} fusion(bf16[256,1536]{1,0:T(8,128)(2,1)} %param.18, bf16[2048,1536]{1,0:T(8,128)(2,1)} %all-gather.3.cloned.1.call-done, bf16[1536,256]{1,0:T(8,128)(2,1)} %param.17, f32[2048,256]{1,0:T(8,128)} %fusion.71), kind=kOutput, calls=%fused_computation.14 | convolution fusion | flops 3224371200 | bytes 22544384 | tf_op jit(solution)/shard_map/dot_general | solution.py:69
  97.3 0.7 copy.75
  98.2 1.8 scatter_custom_fusion
  100.0 8.3 %all-to-all-start = ((s32[128,2,3]{2,1,0:T(2,128)}), s32[128,2,3]{2,1,0:T(2,128)}, u32[]{:S(2)}, u32[]{:S(2)}) async-start(s32[128,2,3]{2,1,0:T(2,128)} %bitcast.80), calls=%async_computation | async-start | bytes 262144 | tf_op jit(solution)/shard_map/all_to_all | solution.py:98
  109.6 8.5 %all-to-all-done = s32[128,2,3]{2,1,0:T(2,128)} async-done(((s32[128,2,3]{2,1,0:T(2,128)}), s32[128,2,3]{2,1,0:T(2,128)}, u32[]{:S(2)}, u32[]{:S(2)}) %all-to-all-start) | async-done | bytes 3104 | tf_op jit(solution)/shard_map/all_to_all | solution.py:98
  118.1 1.0 copy.93
  119.1 73.2 %reduce-scatter.2.cloned.1.call-done = f32[128,1536]{1,0:T(8,128)} async-done(((f32[2048,1536]{1,0:T(8,128)}), f32[128,1536]{1,0:T(8,128)}) %reduce-scatter.2.cloned.1.call-update) | async-done | bytes 786448 | tf_op jit(solution)/shard_map/reduce_scatter | solution.py:68
  192.3 1.4 fusion.39
  193.7 1.5 multiply_reduce_fusion.1
  195.2 3.3 %convolution_convert_fusion.1 = bf16[128,768]{1,0:T(8,128)(2,1)} fusion(bf16[1536,768]{1,0:T(8,128)(2,1)} %param.21, f32[1536]{0:T(1024)} %param.20, f32[128]{0:T(128)S(1)} %add_rsqrt_fusion.1, f32[128]{0:T(128)S(1)} %broadcast_multiply_fusion.1, bf16[128,1536]{1,0:T(8,128)(2,1)} %param.14, f32[128,1536]{1,0:T(8,128)} %reduce-scatter.2.cloned.1.call-done, ...), kind=kOutput, calls=%fused_computation.25 | convolution fusion | flops 303464448 | bytes 3748864 | tf_op jit(solution)/shard_map/dot_general | solution.py:76
  198.5 2.3 scatter_custom_fusion.1
  200.7 1.9 reshape.196
  202.6 7.8 %all-to-all-start.1 = ((bf16[128,2,768]{2,1,0:T(2,128)(2,1)}), bf16[128,2,768]{2,1,0:T(2,128)(2,1)}, u32[]{:S(2)}, u32[]{:S(2)}) async-start(bf16[128,2,768]{2,1,0:T(2,128)(2,1)} %reshape.196), calls=%async_computation.2 | async-start | bytes 786432 | tf_op jit(solution)/shard_map/all_to_all | solution.py:91
  211.0 2.2 scatter_custom_fusion.3
  213.2 1.1 fusion.52
  214.3 2.5 multiply_sine_fusion.1
  216.8 5.7 %all-to-all-done.1 = bf16[128,2,768]{2,1,0:T(2,128)(2,1)} async-done(((bf16[128,2,768]{2,1,0:T(2,128)(2,1)}), bf16[128,2,768]{2,1,0:T(2,128)(2,1)}, u32[]{:S(2)}, u32[]{:S(2)}) %all-to-all-start.1) | async-done | bytes 393248 | tf_op jit(solution)/shard_map/all_to_all | solution.py:91
  222.5 1.9 reshape.226
  224.3 2.7 scatter_custom_fusion.2
  227.0 1.4 fusion.66
  230.2 1.7 copy-done.7
  231.9 0.9 reshape.201
  233.1 0.7 reshape.202
  233.9 4.4 %all-to-all-start.2 = ((bf16[8,128,1536]{2,1,0:T(8,128)(2,1)}), bf16[8,128,1536]{2,1,0:T(8,128)(2,1)S(1)}, u32[]{:S(2)}, u32[]{:S(2)}) async-start(bf16[8,128,1536]{2,1,0:T(8,128)(2,1)} %bitcast.76), calls=%async_computation.3 | async-start | bytes 6291456 | tf_op jit(solution)/shard_map/all_to_all | solution.py:124
  239.1 0.9 slice.53
  240.2 1.1 reshape.200
  241.3 1.9 select_reduce_fusion.1
  243.2 34.0 %all-to-all-done.2 = bf16[8,128,1536]{2,1,0:T(8,128)(2,1)S(1)} async-done(((bf16[8,128,1536]{2,1,0:T(8,128)(2,1)}), bf16[8,128,1536]{2,1,0:T(8,128)(2,1)S(1)}, u32[]{:S(2)}, u32[]{:S(2)}) %all-to-all-start.2) | async-done | bytes 3145760 | tf_op jit(solution)/shard_map/all_to_all | solution.py:124
  277.2 1.9 fusion.68
  279.1 1.8 copy.95
  281.0 1.7 copy.96
  282.6 1.1 multiply_reduce_fusion
  283.7 2.7 copy-done.3
  286.4 1.9 fusion.1
  288.3 10.6 %all-gather.5.cloned.1.call-done = bf16[1024,1536]{1,0:T(8,128)(2,1)} async-done(((bf16[8,1536]{1,0:T(8,128)(2,1)}), bf16[1024,1536]{1,0:T(8,128)(2,1)}) %all-gather.5.cloned.1.call-update) | async-done | bytes 3145744 | tf_op jit(solution)/shard_map/all_gather | solution.py:144
  298.9 3.2 fusion.67
  302.1 1.7 copy.83
  303.8 1.2 fusion.70
  306.6 0.7 copy.86
  307.4 1.3 fusion.15
  308.7 1.0 copy.89
  309.8 4.8 %fusion.26 = bf16[128,12,64]{0,2,1:T(8,128)(2,1)S(1)} fusion(bf16[1024,12,64]{0,2,1:T(8,128)(2,1)} %bitcast.78, f32[12,128,1024]{2,1,0:T(8,128)} %copy-done.3, f32[12,128]{1,0:T(8,128)S(1)} %get-tuple-element.25, f32[128,12,64]{0,2,1:T(8,128)} %copy.89, f32[128,12]{0,1:T(8,128)S(1)} %get-tuple-element.8, f32[128,12]{0,1:T(8,128)} %bitcast.83, ...), kind=kOutput, calls=%fused_computation.33 | convolution fusion | flops 206635008 | bytes 8480256 | tf_op jit(solution)/shard_map/hqk,khd->qhd/dot_general | solution.py:37
  314.6 1.0 fusion.14
  (77 shorter events, 7.5 us)
Async XLA Ops:
  6.5 222.1 %copy-start = (bf16[768,2304]{1,0:T(8,128)(2,1)S(1)}, bf16[768,2304]{1,0:T(8,128)(2,1)}, u32[]{:S(2)}) copy-start(bf16[768,2304]{1,0:T(8,128)(2,1)} %param.25) | copy-start | bytes 10616836
  6.5 69.4 %all-gather.3.cloned.1.call-start = ((), (), s32[]{:S(2)}) async-start(), calls=%async_computation.4 | async-start | bytes 6684672 | tf_op jit(solution)/shard_map/all_gather | solution.py:64
  11.1 181.2 %reduce-scatter.2.cloned.1.call-start = ((), (), s32[]{:S(2)}) async-start(), calls=%async_computation.5 | async-start | bytes 13369344 | tf_op jit(solution)/shard_map/reduce_scatter | solution.py:68
  96.6 0.7 copy-start.15
  96.6 0.7 copy-start.17
  96.6 95.7 %copy-start.9 = (f32[1536]{0:T(1024)S(1)}, f32[1536]{0:T(1024)}, u32[]{:S(2)}) copy-start(f32[1536]{0:T(1024)} %param.19) | copy-start | bytes 18436
  98.2 1.8 copy-start.18
  100.0 18.1 %all-to-all-start = ((s32[128,2,3]{2,1,0:T(2,128)}), s32[128,2,3]{2,1,0:T(2,128)}, u32[]{:S(2)}, u32[]{:S(2)}) async-start(s32[128,2,3]{2,1,0:T(2,128)} %bitcast.80), calls=%async_computation | async-start | bytes 262144 | tf_op jit(solution)/shard_map/all_to_all | solution.py:98
  198.5 30.2 %copy-start.14 = (f32[768]{0:T(1024)S(1)}, f32[768]{0:T(1024)}, u32[]{:S(2)}) copy-start(f32[768]{0:T(1024)} %param.24) | copy-start | bytes 9220
  202.6 19.8 %all-to-all-start.1 = ((bf16[128,2,768]{2,1,0:T(2,128)(2,1)}), bf16[128,2,768]{2,1,0:T(2,128)(2,1)}, u32[]{:S(2)}, u32[]{:S(2)}) async-start(bf16[128,2,768]{2,1,0:T(2,128)(2,1)} %reshape.196), calls=%async_computation.2 | async-start | bytes 786432 | tf_op jit(solution)/shard_map/all_to_all | solution.py:91
  210.4 88.5 %all-gather.5.cloned.1.call-start = ((), (), s32[]{:S(2)}) async-start(), calls=%async_computation.6 | async-start | bytes 3170304 | tf_op jit(solution)/shard_map/all_gather | solution.py:144
  210.5 0.5 copy-start.16
  228.5 1.0 copy-start.5
  229.4 0.8 copy-start.2
  230.2 1.7 copy-start.7
  233.9 43.3 %all-to-all-start.2 = ((bf16[8,128,1536]{2,1,0:T(8,128)(2,1)}), bf16[8,128,1536]{2,1,0:T(8,128)(2,1)S(1)}, u32[]{:S(2)}, u32[]{:S(2)}) async-start(bf16[8,128,1536]{2,1,0:T(8,128)(2,1)} %bitcast.76), calls=%async_computation.3 | async-start | bytes 6291456 | tf_op jit(solution)/shard_map/all_to_all | solution.py:124
  279.1 1.9 copy-start.4
  283.7 2.7 copy-start.3
  305.2 0.6 copy-start.10
  307.3 2.4 copy-start.11
  307.3 2.4 copy-start.12
  307.3 2.4 copy-start.13
  309.7 4.9 %copy-start.6 = (f32[128,768]{1,0:T(8,128)S(1)}, f32[128,768]{1,0:T(8,128)}, u32[]{:S(2)}) copy-start(f32[128,768]{1,0:T(8,128)} %copy-done.5) | copy-start | bytes 1179652
  309.7 4.9 %copy-start.8 = (bf16[768,768]{1,0:T(8,128)(2,1)S(1)}, bf16[768,768]{1,0:T(8,128)(2,1)}, u32[]{:S(2)}) copy-start(bf16[768,768]{1,0:T(8,128)(2,1)} %param.27) | copy-start | bytes 3538948
  309.8 5.9 %copy-start.1 = (bf16[768,2304]{1,0:T(8,128)(2,1)S(1)}, bf16[768,2304]{1,0:T(8,128)(2,1)}, u32[]{:S(2)}) copy-start(bf16[768,2304]{1,0:T(8,128)(2,1)} %param.25) | copy-start | bytes 10616836
Sparse Core Ops, SparseCore 0:
  11.3 64.6 all-gather.2
  96.7 95.5 reduce-scatter.1
  234.0 64.8 all-gather.4
